TPU v7x, 32 devices: a whole 2x2x4 slice. The times are simulated.
32 devices in a mesh: groups: 2 (over x), blk: 16 (over z, y, core).
Axes of the slice: x: 2, y: 2, z: 4, core: 2. Of those that a mesh axis runs over, the one named last changes fastest.
Arguments:
- embeddings: bfloat16 [16384, 1024], P(('groups', 'blk')), parts along dimension 0, may hold values from -6 to 6
- position: int32 [16384], P(('groups', 'blk')), parts along dimension 0, may hold values from 0 to 8191, as said below
- member: int32 [16384], P(('groups', 'blk')), parts along dimension 0, may hold values from 0 to 8191, as said below
- cluster: int32 [16384], P('groups'), parts along dimension 0, may hold values from 0 to 32, as said below
Outputs:
- smoothed: bfloat16 [16384, 1024], P(('groups', 'blk')), parts along dimension 0
- soft_count: bfloat16 [16384], P(('groups', 'blk')), parts along dimension 0
There are 2 independent parts, one for each index of `groups`. A program takes and returns all parts, laid end to end along the dimension named above; each array names one. Nothing has to cross between parts.
Inputs may be any that keep to these rules, and one draw needn't show every extreme that they name: `position`: A permutation; of the rows of one device exactly 32 land in each device's range of 512 places. `member`: the inverse permutation of position. Never falls; ids are consecutive from 0; each cluster holds 1 to 1024 consecutive places and one holds exactly 1024.
All inputs are finite; a program needn't handle non-finite values.
Results may differ from a plain program's by a relative error of at most 0.0065.
Values may be sent and summed in bfloat16 or wider, within the bound.
A program may use at most 64 MiB of HBM per device.

v0:
```python
import jax
import jax.numpy as jnp
from jax import lax
from jax.sharding import PartitionSpec as P

SPAN = 2


SHARPNESS = 32.0
EPSILON = 1e-06


def shifted(block, axis, distance):
    devices = range(lax.axis_size(axis))
    route = [(i - distance, i) for i in devices if i - distance in devices]
    return lax.ppermute(block, axis, route)


def inverse_norm(row_block):
    widened = row_block.astype(jnp.float32)
    return lax.rsqrt(jnp.sum(widened * widened, axis=1) + EPSILON)


def pair_scores(own_rows, own_inverse, own_ids, other_rows, other_inverse, other_ids, same_block):
    products = jnp.einsum("id,jd->ij", own_rows, other_rows, preferred_element_type=jnp.float32)
    cosine = products * own_inverse[:, None] * other_inverse[None, :]
    allowed = own_ids[:, None] == other_ids[None, :]
    if same_block:
        row_places = lax.broadcasted_iota(jnp.int32, allowed.shape, 0)
        col_places = lax.broadcasted_iota(jnp.int32, allowed.shape, 1)
        allowed = allowed & (row_places != col_places)
    return jnp.where(allowed, jax.nn.sigmoid(SHARPNESS * cosine), jnp.float32(0.0))


def local(embeddings, position, member, cluster):
    row_count, feat_width = embeddings.shape
    devices = lax.axis_size("blk")
    my_index = lax.axis_index("blk")
    per_peer = row_count // devices
    sorter = jnp.argsort(position)
    outgoing = embeddings[sorter].reshape(devices, per_peer, feat_width)
    incoming = lax.all_to_all(outgoing, "blk", split_axis=0, concat_axis=0, tiled=True)
    source = member // row_count
    arrange = jnp.argsort(source * row_count + jnp.arange(row_count, dtype=jnp.int32))
    inverse_rank = jnp.argsort(arrange)
    sorted_rows = incoming.reshape(row_count, feat_width)[inverse_rank]
    own_inverse = inverse_norm(sorted_rows)

    def cluster_ids(device):
        inside = (device >= 0) & (device < devices)
        window = lax.dynamic_slice_in_dim(
            cluster, jnp.clip(device, 0, devices - 1) * row_count, row_count, 0
        )
        return jnp.where(inside, window, jnp.int32(-1))

    own_ids = cluster_ids(my_index)
    own_scores = pair_scores(
        sorted_rows, own_inverse, own_ids, sorted_rows, own_inverse, own_ids, True
    )
    summed = jnp.dot(
        own_scores.astype(jnp.bfloat16), sorted_rows, preferred_element_type=jnp.float32
    )
    tallied = jnp.sum(own_scores, axis=1)
    earlier = sorted_rows
    later = sorted_rows
    for distance in range(1, SPAN + 1):
        earlier = shifted(earlier, "blk", 1)
        later = shifted(later, "blk", -1)
        for visitor, visitor_ids in (
            (earlier, cluster_ids(my_index - distance)),
            (later, cluster_ids(my_index + distance)),
        ):
            scores = pair_scores(
                sorted_rows,
                own_inverse,
                own_ids,
                visitor,
                inverse_norm(visitor),
                visitor_ids,
                False,
            )
            weights = scores.astype(jnp.bfloat16)
            term = jnp.dot(weights, visitor, preferred_element_type=jnp.float32)
            rounded = lax.optimization_barrier(term.astype(jnp.bfloat16)).astype(jnp.float32)
            part_tally = jnp.sum(scores, axis=1)
            summed = summed + rounded
            tallied = tallied + part_tally
    smoothed_sorted = (summed / jnp.sqrt(1.0 + tallied)[:, None]).astype(jnp.bfloat16)
    counted_sorted = tallied.astype(jnp.bfloat16)
    returning = smoothed_sorted[arrange].reshape(devices, per_peer, feat_width)
    returning_count = counted_sorted[arrange].reshape(devices, per_peer)
    arrived, arrived_count = (
        lax.all_to_all(returning, "blk", split_axis=0, concat_axis=0, tiled=True),
        lax.all_to_all(returning_count, "blk", split_axis=0, concat_axis=0, tiled=True),
    )
    restore = jnp.argsort(sorter)
    return (
        arrived.reshape(row_count, feat_width)[restore],
        arrived_count.reshape(row_count)[restore],
    )


def solution(mesh):
    in_specs = (P(("groups", "blk"), None), P(("groups", "blk")), P(("groups", "blk")), P("groups"))
    out_specs = (P(("groups", "blk"), None), P(("groups", "blk")))
    return jax.shard_map(local, mesh=mesh, in_specs=in_specs, out_specs=out_specs, check_vma=False)
```

profile of v0, /device:TPU:0, one launch (start us, length us, event | category | flops | bytes accessed | tf_op | source)
XLA Modules:
  0.0 152.2 jit_solution(5144115514035891553)
XLA Ops:
  0.6 0.0 copy-start
  0.7 4.5 %sort.59 = (s32[512]{0:T(512)}, s32[512]{0:T(512)S(1)}) sort(s32[512]{0:T(512)} %param.5, s32[512]{0:T(512)S(1)} %iota.28), dimensions={0}, to_apply=%region_0.0 | sort | flops 4608 | bytes 8192 | tf_op jit(solution)/shard_map/jit(argsort)/sort | solution.py:40
  5.2 0.0 copy-done
  5.2 2.8 %gather_fusion = bf16[512,1024]{1,0:T(8,128)(2,1)} fusion(bf16[512,1024]{1,0:T(8,128)(2,1)S(1)} %copy-done, s32[1024]{0:T(1024)S(1)} %pad_clamp_fusion.3), kind=kCustom, calls=%fused_computation | custom fusion | bytes 2099200 | tf_op jit(solution)/shard_map/gather | solution.py:41
  8.0 7.5 %all-to-all-start = ((bf16[16,32,1024]{2,1,0:T(8,128)(2,1)}), bf16[16,32,1024]{2,1,0:T(8,128)(2,1)S(1)}, u32[]{:S(2)}, u32[]{:S(2)}) async-start(bf16[16,32,1024]{2,1,0:T(8,128)(2,1)} %bitcast), calls=%async_computation | async-start | bytes 2097152 | tf_op jit(solution)/shard_map/all_to_all | solution.py:42
  15.5 0.0 copy-done.2
  15.6 3.8 %sort.60 = (s32[512]{0:T(512)}, s32[512]{0:T(512)S(1)}) sort(s32[512]{0:T(512)S(1)} %fusion.44, s32[512]{0:T(512)S(1)} %iota.30), dimensions={0}, to_apply=%region_1.2 | sort | flops 4608 | bytes 8192 | tf_op jit(solution)/shard_map/jit(argsort)/sort | solution.py:44
  19.4 3.8 %sort.61 = (s32[512]{0:T(512)}, s32[512]{0:T(512)S(1)}) sort(s32[512]{0:T(512)S(1)} %get-tuple-element.7, s32[512]{0:T(512)S(1)} %iota.31), dimensions={0}, to_apply=%region_2.3 | sort | flops 4608 | bytes 8192 | tf_op jit(solution)/shard_map/jit(argsort)/sort | solution.py:45
  23.2 0.9 dynamic-slice_select_fusion.3
  24.1 14.3 %all-to-all-done = bf16[16,32,1024]{2,1,0:T(8,128)(2,1)S(1)} async-done(((bf16[16,32,1024]{2,1,0:T(8,128)(2,1)}), bf16[16,32,1024]{2,1,0:T(8,128)(2,1)S(1)}, u32[]{:S(2)}, u32[]{:S(2)}) %all-to-all-start) | async-done | bytes 1048608 | tf_op jit(solution)/shard_map/all_to_all | solution.py:42
  38.5 2.0 %gather_fusion.1 = bf16[512,1024]{1,0:T(8,128)(2,1)S(1)} fusion(bf16[512,1024]{1,0:T(8,128)(2,1)S(1)} %bitcast.24, s32[1024]{0:T(1024)S(1)} %pad_clamp_fusion.2), kind=kCustom, calls=%fused_computation.1 | custom fusion | bytes 2099200 | tf_op jit(solution)/shard_map/gather | solution.py:46
  40.5 1.3 collective-permute-start.1
  41.8 3.2 %collective-permute-start = (bf16[512,1024]{1,0:T(8,128)(2,1)S(1)}, bf16[512,1024]{1,0:T(8,128)(2,1)S(1)}, u32[]{:S(2)}, u32[]{:S(2)}) collective-permute-start(bf16[512,1024]{1,0:T(8,128)(2,1)S(1)} %gather_fusion.1), channel_id=1, source_target_pairs={{0,1},{1,2},{2,3},{3,4},{4,5},{5,6},{6,7},{7,8},{8,9},{9,10},{10,1... | collective-permute-start | bytes 3145736 | tf_op jit(solution)/shard_map/ppermute | solution.py:16
  45.0 0.3 multiply_reduce_fusion.4
  45.3 1.1 fusion.50
  46.4 2.1 %fusion.40 = f32[512,1024]{1,0:T(8,128)} fusion(bf16[512,1024]{1,0:T(8,128)(2,1)S(1)} %gather_fusion.1, bf16[512,512]{0,1:T(8,128)(2,1)S(1)} %get-tuple-element.24), kind=kOutput, calls=%fused_computation.62 | convolution fusion | flops 536870912 | bytes 3670016 | tf_op jit(solution)/shard_map/dot_general | solution.py:60
  48.5 0.0 collective-permute-done.1
  48.5 0.3 multiply_reduce_fusion.2
  48.8 1.0 fusion.49
  49.8 1.7 %convolution_convert_fusion.2 = bf16[512,1024]{1,0:T(8,128)(2,1)} fusion(bf16[512,1024]{1,0:T(8,128)(2,1)S(1)} %collective-permute-done.1, bf16[512,512]{0,1:T(8,128)(2,1)S(1)} %get-tuple-element.22), kind=kOutput, calls=%fused_computation.14 | convolution fusion | flops 537395200 | bytes 2621440 | tf_op jit(solution)/shard_map/dot_general | solution.py:83
  51.5 1.3 collective-permute-start.3
  52.8 0.0 collective-permute-done
  52.8 0.3 multiply_reduce_fusion.3
  53.1 1.0 fusion.51
  54.0 1.7 %convolution_convert_fusion.3 = bf16[512,1024]{1,0:T(8,128)(2,1)} fusion(bf16[512,1024]{1,0:T(8,128)(2,1)S(1)} %collective-permute-done, bf16[512,512]{0,1:T(8,128)(2,1)S(1)} %get-tuple-element.26), kind=kOutput, calls=%fused_computation.15 | convolution fusion | flops 537395200 | bytes 2621440 | tf_op jit(solution)/shard_map/dot_general | solution.py:83
  55.8 29.7 %collective-permute-start.2 = (bf16[512,1024]{1,0:T(8,128)(2,1)S(1)}, bf16[512,1024]{1,0:T(8,128)(2,1)S(1)}, u32[]{:S(2)}, u32[]{:S(2)}) collective-permute-start(bf16[512,1024]{1,0:T(8,128)(2,1)S(1)} %collective-permute-done), channel_id=1, source_target_pairs={{0,1},{1,2},{2,3},{3,4},{4,5},{5,6},{6,7},{7,8},{8,9},{9,10},{10,1... | collective-permute-start | bytes 3145736 | tf_op jit(solution)/shard_map/ppermute | solution.py:16
  85.5 0.0 collective-permute-done.3
  85.5 0.3 multiply_reduce_fusion
  85.8 1.0 fusion.47
  86.8 1.7 %convolution_convert_fusion = bf16[512,1024]{1,0:T(8,128)(2,1)} fusion(bf16[512,1024]{1,0:T(8,128)(2,1)S(1)} %collective-permute-done.3, bf16[512,512]{0,1:T(8,128)(2,1)S(1)} %get-tuple-element.18), kind=kOutput, calls=%fused_computation.12 | convolution fusion | flops 537395200 | bytes 2621440 | tf_op jit(solution)/shard_map/dot_general | solution.py:83
  88.5 0.0 collective-permute-done.2
  88.5 0.3 multiply_reduce_fusion.1
  88.8 1.0 fusion.48
  89.8 0.0 copy-start.1
  89.8 1.7 %convolution_convert_fusion.1 = bf16[512,1024]{1,0:T(8,128)(2,1)} fusion(bf16[512,1024]{1,0:T(8,128)(2,1)S(1)} %collective-permute-done.2, bf16[512,512]{0,1:T(8,128)(2,1)S(1)} %get-tuple-element.20), kind=kOutput, calls=%fused_computation.13 | convolution fusion | flops 537395200 | bytes 2621440 | tf_op jit(solution)/shard_map/dot_general | solution.py:83
  91.5 3.5 %gather_fusion.4 = bf16[512]{0:T(512)(128)(2,1)S(1)} fusion(bf16[512]{0:T(512)(128)(2,1)S(1)} %get-tuple-element.10, s32[1024]{0:T(1024)S(1)} %pad_clamp_fusion.1), kind=kCustom, calls=%fused_computation.4 | custom fusion | bytes 4096 | tf_op jit(solution)/shard_map/gather | solution.py:91
  95.1 0.7 all_to_all.16
  95.7 18.3 %all-to-all-start.2 = ((bf16[16,1,32]{2,1,0:T(2,128)(2,1)}), bf16[16,1,32]{2,1,0:T(2,128)(2,1)S(1)}, u32[]{:S(2)}, u32[]{:S(2)}) async-start(bf16[16,1,32]{2,1,0:T(2,128)(2,1)} %all_to_all.16), calls=%async_computation.2 | async-start | bytes 16384 | tf_op jit(solution)/shard_map/all_to_all | solution.py:94
  114.1 0.0 copy-done.1
  114.1 3.6 %divide_convert_fusion = bf16[512,1024]{1,0:T(8,128)(2,1)S(1)} fusion(bf16[512,1024]{1,0:T(8,128)(2,1)} %convolution_convert_fusion, bf16[512,1024]{1,0:T(8,128)(2,1)} %convolution_convert_fusion.1, bf16[512,1024]{1,0:T(8,128)(2,1)S(1)} %copy-done.1, f32[512,1024]{1,0:T(8,128)} %fusion.40, bf16[512,1024]{1,0:T(8,128)(2,1)} %convolution_convert_fusion.3, ...), kind=kLoop, calls=%fused_computation.6 | loop fusion | flops 5242880 | bytes 7342080 | tf_op jit(solution)/shard_map/convert_element_type | solution.py:88
  117.7 2.8 %gather_fusion.2 = bf16[512,1024]{1,0:T(8,128)(2,1)} fusion(bf16[512,1024]{1,0:T(8,128)(2,1)S(1)} %divide_convert_fusion, s32[1024]{0:T(1024)S(1)} %pad_clamp_fusion.1), kind=kCustom, calls=%fused_computation.2 | custom fusion | bytes 2099200 | tf_op jit(solution)/shard_map/gather | solution.py:90
  120.4 0.0 all-to-all-done.2
  120.5 6.0 %all-to-all-start.1 = ((bf16[16,32,1024]{2,1,0:T(8,128)(2,1)}), bf16[16,32,1024]{2,1,0:T(8,128)(2,1)S(1)}, u32[]{:S(2)}, u32[]{:S(2)}) async-start(bf16[16,32,1024]{2,1,0:T(8,128)(2,1)} %bitcast.2), calls=%async_computation.1 | async-start | bytes 2097152 | tf_op jit(solution)/shard_map/all_to_all | solution.py:93
  126.5 3.8 %sort.62 = (s32[512]{0:T(512)}, s32[512]{0:T(512)S(1)}) sort(s32[512]{0:T(512)S(1)} %get-tuple-element.6, s32[512]{0:T(512)S(1)} %iota.32), dimensions={0}, to_apply=%region_13.14 | sort | flops 4608 | bytes 8192 | tf_op jit(solution)/shard_map/jit(argsort)/sort | solution.py:96
  130.3 0.1 reshape.74
  130.4 4.6 %gather_fusion.5 = bf16[512]{0:T(512)(128)(2,1)} fusion(bf16[512]{0:T(512)(128)(2,1)S(1)} %reshape.74, s32[1024]{0:T(1024)S(1)} %pad_clamp_fusion), kind=kCustom, calls=%fused_computation.5 | custom fusion | bytes 4096 | tf_op jit(solution)/shard_map/gather | solution.py:99
  135.0 14.4 %all-to-all-done.1 = bf16[16,32,1024]{2,1,0:T(8,128)(2,1)S(1)} async-done(((bf16[16,32,1024]{2,1,0:T(8,128)(2,1)}), bf16[16,32,1024]{2,1,0:T(8,128)(2,1)S(1)}, u32[]{:S(2)}, u32[]{:S(2)}) %all-to-all-start.1) | async-done | bytes 1048608 | tf_op jit(solution)/shard_map/all_to_all | solution.py:93
  149.4 2.8 %gather_fusion.3 = bf16[512,1024]{1,0:T(8,128)(2,1)} fusion(bf16[512,1024]{1,0:T(8,128)(2,1)S(1)} %bitcast.25, s32[1024]{0:T(1024)S(1)} %pad_clamp_fusion), kind=kCustom, calls=%fused_computation.3 | custom fusion | bytes 2099200 | tf_op jit(solution)/shard_map/gather | solution.py:98
  (22 shorter events, 0.2 us)
Async XLA Ops:
  0.6 4.6 %copy-start = (bf16[512,1024]{1,0:T(8,128)(2,1)S(1)}, bf16[512,1024]{1,0:T(8,128)(2,1)}, u32[]{:S(2)}) copy-start(bf16[512,1024]{1,0:T(8,128)(2,1)} %param.4) | copy-start | bytes 3145732
  8.0 7.6 %copy-start.2 = (s32[512]{0:T(512)S(1)}, s32[512]{0:T(512)}, u32[]{:S(2)}) copy-start(s32[512]{0:T(512)} %param.6) | copy-start | bytes 6148
  8.0 30.5 %all-to-all-start = ((bf16[16,32,1024]{2,1,0:T(8,128)(2,1)}), bf16[16,32,1024]{2,1,0:T(8,128)(2,1)S(1)}, u32[]{:S(2)}, u32[]{:S(2)}) async-start(bf16[16,32,1024]{2,1,0:T(8,128)(2,1)} %bitcast), calls=%async_computation | async-start | bytes 2097152 | tf_op jit(solution)/shard_map/all_to_all | solution.py:42
  40.5 8.0 %collective-permute-start.1 = (bf16[512,1024]{1,0:T(8,128)(2,1)S(1)}, bf16[512,1024]{1,0:T(8,128)(2,1)S(1)}, u32[]{:S(2)}, u32[]{:S(2)}) collective-permute-start(bf16[512,1024]{1,0:T(8,128)(2,1)S(1)} %gather_fusion.1), channel_id=1, source_target_pairs={{1,0},{2,1},{3,2},{4,3},{5,4},{6,5},{7,6},{8,7},{9,8},{10,9},{11,1... | collective-permute-start | bytes 3145736 | tf_op jit(solution)/shard_map/ppermute | solution.py:16
  41.8 11.0 %collective-permute-start = (bf16[512,1024]{1,0:T(8,128)(2,1)S(1)}, bf16[512,1024]{1,0:T(8,128)(2,1)S(1)}, u32[]{:S(2)}, u32[]{:S(2)}) collective-permute-start(bf16[512,1024]{1,0:T(8,128)(2,1)S(1)} %gather_fusion.1), channel_id=1, source_target_pairs={{0,1},{1,2},{2,3},{3,4},{4,5},{5,6},{6,7},{7,8},{8,9},{9,10},{10,1... | collective-permute-start | bytes 3145736 | tf_op jit(solution)/shard_map/ppermute | solution.py:16
  51.5 34.0 %collective-permute-start.3 = (bf16[512,1024]{1,0:T(8,128)(2,1)S(1)}, bf16[512,1024]{1,0:T(8,128)(2,1)S(1)}, u32[]{:S(2)}, u32[]{:S(2)}) collective-permute-start(bf16[512,1024]{1,0:T(8,128)(2,1)S(1)} %collective-permute-done.1), channel_id=1, source_target_pairs={{1,0},{2,1},{3,2},{4,3},{5,4},{6,5},{7,6},{8,7},{9,8},{10,9},{11,1... | collective-permute-start | bytes 3145736 | tf_op jit(solution)/shard_map/ppermute | solution.py:16
  55.8 32.7 %collective-permute-start.2 = (bf16[512,1024]{1,0:T(8,128)(2,1)S(1)}, bf16[512,1024]{1,0:T(8,128)(2,1)S(1)}, u32[]{:S(2)}, u32[]{:S(2)}) collective-permute-start(bf16[512,1024]{1,0:T(8,128)(2,1)S(1)} %collective-permute-done), channel_id=1, source_target_pairs={{0,1},{1,2},{2,3},{3,4},{4,5},{5,6},{6,7},{7,8},{8,9},{9,10},{10,1... | collective-permute-start | bytes 3145736 | tf_op jit(solution)/shard_map/ppermute | solution.py:16
  89.8 24.3 %copy-start.1 = (bf16[512,1024]{1,0:T(8,128)(2,1)S(1)}, bf16[512,1024]{1,0:T(8,128)(2,1)}, u32[]{:S(2)}) copy-start(bf16[512,1024]{1,0:T(8,128)(2,1)} %convolution_convert_fusion.2) | copy-start | bytes 3145732
  95.7 24.7 %all-to-all-start.2 = ((bf16[16,1,32]{2,1,0:T(2,128)(2,1)}), bf16[16,1,32]{2,1,0:T(2,128)(2,1)S(1)}, u32[]{:S(2)}, u32[]{:S(2)}) async-start(bf16[16,1,32]{2,1,0:T(2,128)(2,1)} %all_to_all.16), calls=%async_computation.2 | async-start | bytes 16384 | tf_op jit(solution)/shard_map/all_to_all | solution.py:94
  120.5 28.9 %all-to-all-start.1 = ((bf16[16,32,1024]{2,1,0:T(8,128)(2,1)}), bf16[16,32,1024]{2,1,0:T(8,128)(2,1)S(1)}, u32[]{:S(2)}, u32[]{:S(2)}) async-start(bf16[16,32,1024]{2,1,0:T(8,128)(2,1)} %bitcast.2), calls=%async_computation.1 | async-start | bytes 2097152 | tf_op jit(solution)/shard_map/all_to_all | solution.py:93
where the time goes:
time: 154 us; the launch traced here: 152 us
  starting transfers between devices  67.3 us (44%)
  waiting for transfers between devices  28.8 us (19%)
  other arithmetic  21.9 us (14%)
  local copies, waits for them, and re-layouts  19.3 us (13%)
  matrix products  14 us (9%)
    ppermute x4, starting transfers between devices, shifted(): return lax.ppermute(block, axis, route)  35.5 us
    all_to_all x1, starting transfers between devices, local(): lax.all_to_all(returning_count, 'blk', split_axis=0, concat_axis=0, tiled...  18.3 us
    all_to_all x1, waiting for transfers between devices, local(): lax.all_to_all(returning, 'blk', split_axis=0, concat_axis=0, tiled=True)  14.4 us
    all_to_all x1, waiting for transfers between devices, local(): lax.all_to_all(outgoing, 'blk', split_axis=0, concat_axis=0, tiled=True)  14.3 us
    all_to_all x1, starting transfers between devices, local(): lax.all_to_all(outgoing, 'blk', split_axis=0, concat_axis=0, tiled=True)  7.52 us
    dot_general x4, matrix products, local(): term = jnp.dot(weights, visitor, preferred_element_type=jnp.float32)  6.88 us
    all_to_all x1, starting transfers between devices, local(): lax.all_to_all(returning, 'blk', split_axis=0, concat_axis=0, tiled=True)  5.97 us
    dot_general x5, matrix products, pair_scores(): jnp.einsum('id,jd->ij', own_rows, other_rows, preferred_element_type=jnp....  5.02 us
  transfers between devices with their start and end apart: 7, of which 2 were waited for; matrix products, arithmetic and copies ran while one was open for 24% of the time, Pallas kernels for 0%

commit v1 on v0

v1 whole, which is shorter than its diff:
```python
import functools

import jax
import jax.numpy as jnp
from jax import lax
from jax.experimental import pallas as pl
from jax.experimental.pallas import tpu as pltpu
from jax.sharding import PartitionSpec as P

SHARPNESS = 32.0
EPSILON = 1e-06
TILE = 256
F32 = jnp.float32
BF16 = jnp.bfloat16


def snake(device, devices):
    if devices != 16:
        return device
    z, y, core = device // 4, (device // 2) % 2, device % 2
    turn = z % 2
    return z * 4 + (y + turn - 2 * y * turn) * 2 + core


def as_column(row):
    return jnp.transpose(jnp.broadcast_to(row, (128, row.shape[1])))[:, :1]


def as_row(column):
    return jnp.transpose(jnp.broadcast_to(column, (column.shape[0], 128)))[:1, :]


def ones_where(condition):
    return jnp.where(condition, 1.0, 0.0)


def kernel(
    devices, slab, emb, pos, mem, ids, out, count_out,
    outgoing, incoming, own, mate, prev, after, relayed, total, result, returning, returned,
    tallies, tally_table, send_col, place_col, own_inv, own_ids, tally, mem_in,
    mem_sems, out_send, out_recv, win_send, win_recv, back_send, back_recv, tal_send, tal_recv,
):
    rows, width = emb.shape
    slots = devices * slab
    per_peer = rows // devices
    me = lax.axis_index("blk")
    block = snake(me, devices)
    chip, core = block // 2, block % 2
    chips = devices // 2

    def dev(b):
        return {"blk": b}

    def remote(src, dst, send, recv, target):
        return pltpu.make_async_remote_copy(
            src_ref=src, dst_ref=dst, send_sem=send, recv_sem=recv,
            device_id=dev(target), device_id_type=pl.DeviceIdType.MESH,
        )

    def at_slab(ref, index):
        return ref.at[pl.ds(pl.multiple_of(index * slab, slab), slab)]

    barrier = pltpu.get_barrier_semaphore()

    @pl.loop(1, devices)
    def _(k):
        pl.semaphore_signal(
            barrier, inc=1, device_id=dev((me + k) % devices),
            device_id_type=pl.DeviceIdType.MESH,
        )

    pos_row = pos[...].astype(F32)
    pos_col = as_column(pos_row)
    rank = jnp.sum(ones_where(pos_col < pos_row), axis=0, keepdims=True)
    block_row = lax.shift_right_logical(pos[...], (rows - 1).bit_length()).astype(F32)
    send_row = rank + block_row * (slab - per_peer)
    send_col[...] = as_column(send_row)

    @pl.loop(0, slots // TILE)
    def _(t):
        start = pl.multiple_of(t * TILE, TILE)
        places = (lax.broadcasted_iota(jnp.int32, (TILE, rows), 0) + start).astype(F32)
        pick = ones_where(places == send_row).astype(BF16)
        outgoing[pl.ds(start, TILE), :] = jnp.dot(
            pick, emb[...], preferred_element_type=F32
        ).astype(BF16)

    pl.semaphore_wait(barrier, devices - 1)

    def out_copy(k):
        peer = (me + k) % devices
        return remote(
            at_slab(outgoing, snake(peer, devices)), at_slab(incoming, me),
            out_send.at[k], out_recv.at[k], peer,
        )

    def mem_copy():
        return remote(mem, mem_in, mem_sems.at[0], mem_sems.at[1], block)

    @pl.when(block != me)
    def _():
        mem_copy().start()

    @pl.loop(1, devices)
    def _(k):
        out_copy(k).start()

    at_slab(incoming, me)[...] = at_slab(outgoing, block)[...]

    @pl.when(block == me)
    def _():
        mem_in[...] = mem[...]

    @pl.when(block != me)
    def _():
        mem_copy().wait()

    src_row = lax.shift_right_logical(mem_in[...], (rows - 1).bit_length()).astype(F32)
    src_col = as_column(src_row)
    earlier = lax.broadcasted_iota(jnp.int32, (rows, rows), 0) < lax.broadcasted_iota(
        jnp.int32, (rows, rows), 1
    )
    before = jnp.sum(ones_where((src_col == src_row) & earlier), axis=0, keepdims=True)
    place_row = src_row * slab + before
    place_col[...] = as_column(place_row)
    own_ids[...] = as_column(ids[block].astype(F32))

    @pl.loop(1, devices)
    def _(k):
        out_copy(k).wait_recv()

    @pl.loop(0, rows // TILE)
    def _(t):
        part = pl.ds(pl.multiple_of(t * TILE, TILE), TILE)
        lanes = lax.broadcasted_iota(jnp.int32, (TILE, slots), 1).astype(F32)
        pick = ones_where(lanes == place_col[part, :]).astype(BF16)
        own[part, :] = jnp.dot(pick, incoming[...], preferred_element_type=F32).astype(BF16)

    mate_dev = snake(block + 1 - 2 * core, devices)
    has_prev, has_after = chip > 0, chip < chips - 1
    prev_dev = snake(jnp.maximum(block - 2, 0), devices)
    after_dev = snake(jnp.minimum(block + 2, devices - 1), devices)

    def to_mate():
        return remote(own, mate, win_send.at[0], win_recv.at[0], mate_dev)

    def to_after():
        return remote(own, prev, win_send.at[1], win_recv.at[1], after_dev)

    def to_prev():
        return remote(own, after, win_send.at[2], win_recv.at[2], prev_dev)

    def relay(source):
        return remote(source, relayed, win_send.at[3], win_recv.at[3], mate_dev)

    @pl.when(has_after)
    def _():
        to_after().start()

    @pl.when(has_prev)
    def _():
        to_prev().start()

    to_mate().start()

    def inverse(ref):
        widened = ref[...].astype(F32)
        return lax.rsqrt(jnp.sum(widened * widened, axis=1, keepdims=True) + EPSILON)

    def visit(other, other_inv_row, other_block, first):
        other_ids = ids[other_block].astype(F32)

        @pl.loop(0, rows // TILE)
        def _(t):
            start = pl.multiple_of(t * TILE, TILE)
            part = pl.ds(start, TILE)
            products = lax.dot_general(
                own[part, :], other[...], (((1,), (1,)), ((), ())), preferred_element_type=F32
            )
            half = products * (own_inv[part, :] * (0.5 * SHARPNESS)) * other_inv_row
            allowed = own_ids[part, :] == other_ids
            if first:
                here = lax.broadcasted_iota(jnp.int32, (TILE, rows), 0) + start
                there = lax.broadcasted_iota(jnp.int32, (TILE, rows), 1)
                allowed = allowed & (here != there)
            scores = jnp.where(allowed, 0.5 + 0.5 * jnp.tanh(half), 0.0)
            term = jnp.dot(scores.astype(BF16), other[...], preferred_element_type=F32)
            counted = jnp.sum(scores, axis=1, keepdims=True)
            if first:
                total[part, :] = term
                tally[part, :] = counted
            else:
                total[part, :] += term
                tally[part, :] += counted

    own_inv[...] = inverse(own)
    visit(own, as_row(own_inv[...]), block, True)
    to_mate().wait_recv()
    visit(mate, as_row(inverse(mate)), block + 1 - 2 * core, False)

    @pl.when(has_prev)
    def _():
        to_after().wait_recv()

        @pl.when(core == 1)
        def _():
            relay(prev).start()

    @pl.when(has_after)
    def _():
        to_prev().wait_recv()

        @pl.when(core == 0)
        def _():
            relay(after).start()

    @pl.when(has_prev)
    def _():
        visit(prev, as_row(inverse(prev)), block - 2, False)

    @pl.when(has_after)
    def _():
        visit(after, as_row(inverse(after)), block + 2, False)

    gets_relay = ((core == 0) & has_prev) | ((core == 1) & has_after)

    @pl.when(gets_relay)
    def _():
        relay(prev).wait_recv()
        visit(relayed, as_row(inverse(relayed)), block - 1 + 2 * core, False)

    scale = lax.rsqrt(1.0 + tally[...])
    result[...] = (total[...] * scale).astype(BF16)
    tallies[block] = as_row(tally[...])

    def tally_copy(k):
        peer = (me + k) % devices
        return remote(
            tallies.at[block], tallies.at[block], tal_send.at[k], tal_recv.at[k], peer
        )

    def back_copy(k):
        peer = (me + k) % devices
        return remote(
            at_slab(returning, peer), at_slab(returned, block),
            back_send.at[k], back_recv.at[k], peer,
        )

    @pl.loop(1, devices)
    def _(k):
        tally_copy(k).start()

    @pl.loop(0, slots // TILE)
    def _(t):
        start = pl.multiple_of(t * TILE, TILE)
        places = (lax.broadcasted_iota(jnp.int32, (TILE, rows), 0) + start).astype(F32)
        pick = ones_where(places == place_row).astype(BF16)
        returning[pl.ds(start, TILE), :] = jnp.dot(
            pick, result[...], preferred_element_type=F32
        ).astype(BF16)

    @pl.loop(1, devices)
    def _(k):
        back_copy(k).start()

    at_slab(returned, block)[...] = at_slab(returning, me)[...]

    @pl.loop(1, devices)
    def _(k):
        tally_copy(k).wait_recv()

    tally_table[...] = jnp.zeros_like(tally_table)

    @pl.loop(0, devices)
    def _(b):
        tally_table[pl.ds(b, 1), :] = tallies[b]

    which = lax.broadcasted_iota(jnp.int32, (128, rows), 0).astype(F32)
    in_block = jnp.dot(
        jnp.transpose(tally_table[...]).astype(BF16),
        ones_where(which == block_row).astype(BF16),
        preferred_element_type=F32,
    )
    inside = pos_row - block_row * rows
    lines = lax.broadcasted_iota(jnp.int32, (rows, rows), 0).astype(F32)
    count_out[...] = jnp.sum(jnp.where(lines == inside, in_block, 0.0), axis=0, keepdims=True)

    @pl.loop(1, devices)
    def _(k):
        back_copy(k).wait_recv()

    @pl.loop(0, rows // TILE)
    def _(t):
        part = pl.ds(pl.multiple_of(t * TILE, TILE), TILE)
        lanes = lax.broadcasted_iota(jnp.int32, (TILE, slots), 1).astype(F32)
        pick = ones_where(lanes == send_col[part, :]).astype(BF16)
        out[part, :] = jnp.dot(pick, returned[...], preferred_element_type=F32).astype(BF16)

    @pl.loop(1, devices)
    def _(k):
        out_copy(k).wait_send()
        tally_copy(k).wait_send()
        back_copy(k).wait_send()

    to_mate().wait_send()

    @pl.when(has_after)
    def _():
        to_after().wait_send()

    @pl.when(has_prev)
    def _():
        to_prev().wait_send()

    @pl.when(((core == 1) & has_prev) | ((core == 0) & has_after))
    def _():
        relay(prev).wait_send()


def local(embeddings, position, member, cluster):
    rows, width = embeddings.shape
    devices = lax.axis_size("blk")
    slab = max(16, rows // devices)
    slots = devices * slab
    vmem = pl.BlockSpec(memory_space=pltpu.VMEM)
    dma = pltpu.SemaphoreType.DMA
    smoothed, counts = pl.pallas_call(
        functools.partial(kernel, devices, slab),
        out_shape=(
            jax.ShapeDtypeStruct((rows, width), BF16),
            jax.ShapeDtypeStruct((1, rows), F32),
        ),
        in_specs=[vmem] * 4,
        out_specs=(vmem, vmem),
        scratch_shapes=[
            pltpu.VMEM((slots, width), BF16),
            pltpu.VMEM((slots, width), BF16),
            pltpu.VMEM((rows, width), BF16),
            pltpu.VMEM((rows, width), BF16),
            pltpu.VMEM((rows, width), BF16),
            pltpu.VMEM((rows, width), BF16),
            pltpu.VMEM((rows, width), BF16),
            pltpu.VMEM((rows, width), F32),
            pltpu.VMEM((rows, width), BF16),
            pltpu.VMEM((slots, width), BF16),
            pltpu.VMEM((slots, width), BF16),
            pltpu.VMEM((devices, 1, rows), F32),
            pltpu.VMEM((128, rows), F32),
            pltpu.VMEM((rows, 1), F32),
            pltpu.VMEM((rows, 1), F32),
            pltpu.VMEM((rows, 1), F32),
            pltpu.VMEM((rows, 1), F32),
            pltpu.VMEM((rows, 1), F32),
            pltpu.VMEM((1, rows), jnp.int32),
            dma((2,)),
            dma((devices,)),
            dma((devices,)),
            dma((4,)),
            dma((4,)),
            dma((devices,)),
            dma((devices,)),
            dma((devices,)),
            dma((devices,)),
        ],
        compiler_params=pltpu.CompilerParams(
            collective_id=0, has_side_effects=True, vmem_limit_bytes=48 * 1024 * 1024
        ),
    )(
        embeddings,
        position.reshape(1, rows),
        member.reshape(1, rows),
        cluster.reshape(devices, 1, rows),
    )
    return smoothed, counts.reshape(rows).astype(BF16)


def solution(mesh):
    in_specs = (P(("groups", "blk"), None), P(("groups", "blk")), P(("groups", "blk")), P("groups"))
    out_specs = (P(("groups", "blk"), None), P(("groups", "blk")))
    return jax.shard_map(local, mesh=mesh, in_specs=in_specs, out_specs=out_specs, check_vma=False)
```

time: 154 us -> 91 us (0.59)
  the two profiles are of different devices: /device:TPU:0 before, /device:TPU:13 now
where the time goes in v1:
time: 91 us; the launch traced here: 90.8 us
  Pallas kernels  85.9 us (94%)
  local copies, waits for them, and re-layouts  3.63 us (4%)
    pallas_call x1, Pallas kernels, local(): pl.pallas_call(functools.partial(kernel, devices, slab), out_shape=(jax.S...  85.9 us
    unnamed x9, local copies, waits for them, and re-layouts  3.63 us

profile of v1, /device:TPU:13, one launch (start us, length us, event | category | flops | bytes accessed | tf_op | source)
XLA Modules:
  0.0 90.8 jit_solution(14517044008186020244)
XLA Ops:
  0.6 0.0 copy-start.3
  0.6 0.0 copy-start.2
  0.7 0.7 copy-done.3
  1.3 0.0 copy-done.2
  1.3 0.0 copy-start
  1.3 1.2 %copy-done = bf16[512,1024]{1,0:T(8,128)(2,1)S(1)} copy-done((bf16[512,1024]{1,0:T(8,128)(2,1)S(1)}, bf16[512,1024]{1,0:T(8,128)(2,1)}, u32[]{:S(2)}) %copy-start) | copy-done | bytes 1048600
  2.6 0.0 copy-start.1
  2.6 0.8 copy-done.1
  3.3 85.9 %shard_map.59 = (bf16[512,1024]{1,0:T(8,128)(2,1)S(1)}, f32[1,512]{1,0:T(1,128)S(1)}) custom-call(bf16[512,1024]{1,0:T(8,128)(2,1)S(1)} %copy-done, s32[1,512]{1,0:T(1,128)S(1)} %bitcast.4, s32[1,512]{1,0:T(1,128)S(1)} %bitcast.5, s32[16,1,512]{2,1,0:T(1,128)S(1)} %bitcast.3), custom_call_target="tpu_custom_call" | custom-call | tf_op jit(solution)/shard_map/pallas_call | solution.py:327
  89.2 0.6 convert_reduce_fusion
  89.8 1.0 %copy.7 = bf16[512,1024]{1,0:T(8,128)(2,1)} copy(bf16[512,1024]{1,0:T(8,128)(2,1)S(1)} %get-tuple-element.8) | data formatting | bytes 2097152
Async XLA Ops:
  0.6 0.7 copy-start.3
  0.6 0.7 copy-start.2
  1.3 1.2 %copy-start = (bf16[512,1024]{1,0:T(8,128)(2,1)S(1)}, bf16[512,1024]{1,0:T(8,128)(2,1)}, u32[]{:S(2)}) copy-start(bf16[512,1024]{1,0:T(8,128)(2,1)} %emb.1) | copy-start | bytes 3145732
  2.6 0.8 copy-start.1

commit v2 on v1

v2 whole, which is shorter than its diff:
```python
import functools

import jax
import jax.numpy as jnp
from jax import lax
from jax.experimental import pallas as pl
from jax.experimental.pallas import tpu as pltpu
from jax.sharding import PartitionSpec as P

SHARPNESS = 32.0
EPSILON = 1e-06
TILE = 256
CHUNKS = 4
F32 = jnp.float32
BF16 = jnp.bfloat16


def snake(device, devices):
    if devices != 16:
        return device
    z, y, core = device // 4, (device // 2) % 2, device % 2
    turn = z % 2
    return z * 4 + (y + turn - 2 * y * turn) * 2 + core


def as_column(row):
    return jnp.transpose(jnp.broadcast_to(row, (128, row.shape[1])))[:, :1]


def as_row(column):
    return jnp.transpose(jnp.broadcast_to(column, (column.shape[0], 128)))[:1, :]


def ones_where(condition):
    return jnp.where(condition, 1.0, 0.0)


def kernel(
    devices, slab, emb_hbm, pos, mem, ids, out, count_out,
    emb, outgoing, incoming, win, weights, returning, returned,
    send_pick, restore_pick, place_pick, return_pick,
    tallies, tally_table, own_inv, own_ids, tally, mem_in,
    emb_sem, mem_sems, out_send, out_recv, win_send, win_recv, back_send, back_recv,
    tal_send, tal_recv,
):
    rows, width = emb.shape
    slots = devices * slab
    per_peer = rows // devices
    piece = width // CHUNKS
    me = lax.axis_index("blk")
    block = snake(me, devices)
    chip, core = block // 2, block % 2
    chips = devices // 2

    def dev(b):
        return {"blk": b}

    def remote(src, dst, send, recv, target):
        return pltpu.make_async_remote_copy(
            src_ref=src, dst_ref=dst, send_sem=send, recv_sem=recv,
            device_id=dev(target), device_id_type=pl.DeviceIdType.MESH,
        )

    def columns(c):
        return pl.ds(c * piece, piece)

    def at_slab(ref, index, c):
        return ref.at[pl.ds(pl.multiple_of(index * slab, slab), slab), columns(c)]

    def in_tiles(count):
        def run(body):
            @pl.loop(0, count // TILE)
            def _(t):
                start = pl.multiple_of(t * TILE, TILE)
                body(start, pl.ds(start, TILE))
        return run

    def permute(pick, source, target, c):
        @in_tiles(target.shape[0])
        def _(start, part):
            target[part, columns(c)] = jnp.dot(
                pick[part, :], source[:, columns(c)], preferred_element_type=F32
            ).astype(BF16)

    def make_picks(to_slot, from_slot, slot_row):
        slot_col = as_column(slot_row)
        places = lax.broadcasted_iota(jnp.int32, (slots, rows), 0).astype(F32)
        to_slot[...] = ones_where(places == slot_row).astype(BF16)
        lanes = lax.broadcasted_iota(jnp.int32, (rows, slots), 1).astype(F32)
        from_slot[...] = ones_where(lanes == slot_col).astype(BF16)

    fetch = pltpu.make_async_copy(emb_hbm, emb, emb_sem)
    fetch.start()
    barrier = pltpu.get_barrier_semaphore()

    @pl.loop(1, devices)
    def _(k):
        pl.semaphore_signal(
            barrier, inc=1, device_id=dev((me + k) % devices),
            device_id_type=pl.DeviceIdType.MESH,
        )

    pos_row = pos[...].astype(F32)
    pos_col = as_column(pos_row)
    rank = jnp.sum(ones_where(pos_col < pos_row), axis=0, keepdims=True)
    block_row = lax.shift_right_logical(pos[...], (rows - 1).bit_length()).astype(F32)
    send_row = rank + block_row * (slab - per_peer)
    make_picks(send_pick, restore_pick, send_row)
    fetch.wait()
    permute(send_pick, emb, outgoing, 0)
    pl.semaphore_wait(barrier, devices - 1)

    def out_copy(k, c):
        peer = (me + k) % devices
        return remote(
            at_slab(outgoing, snake(peer, devices), c), at_slab(incoming, me, c),
            out_send.at[c, k], out_recv.at[c, k], peer,
        )

    def mem_copy():
        return remote(mem, mem_in, mem_sems.at[0], mem_sems.at[1], block)

    @pl.when(block != me)
    def _():
        mem_copy().start()

    for c in range(CHUNKS):
        if c > 0:
            permute(send_pick, emb, outgoing, c)

        @pl.loop(1, devices)
        def _(k):
            out_copy(k, c).start()

        at_slab(incoming, me, c)[...] = at_slab(outgoing, block, c)[...]

    @pl.when(block == me)
    def _():
        mem_in[...] = mem[...]

    @pl.when(block != me)
    def _():
        mem_copy().wait()

    src_row = lax.shift_right_logical(mem_in[...], (rows - 1).bit_length()).astype(F32)
    src_col = as_column(src_row)
    earlier = lax.broadcasted_iota(jnp.int32, (rows, rows), 0) < lax.broadcasted_iota(
        jnp.int32, (rows, rows), 1
    )
    before = jnp.sum(ones_where((src_col == src_row) & earlier), axis=0, keepdims=True)
    make_picks(return_pick, place_pick, src_row * slab + before)
    own_ids[...] = as_column(ids[block].astype(F32))

    mate_dev = snake(block + 1 - 2 * core, devices)
    has_prev, has_after = chip > 0, chip < chips - 1
    prev_dev = snake(jnp.maximum(block - 2, 0), devices)
    after_dev = snake(jnp.minimum(block + 2, devices - 1), devices)
    own, mate, prev, after, relayed = (win.at[pl.ds(j * rows, rows)] for j in range(5))

    def window_copy(source, target, way, c, device):
        return remote(
            source.at[:, columns(c)], target.at[:, columns(c)],
            win_send.at[way, c], win_recv.at[way, c], device,
        )

    def to_mate(c):
        return window_copy(own, mate, 0, c, mate_dev)

    def to_after(c):
        return window_copy(own, prev, 1, c, after_dev)

    def to_prev(c):
        return window_copy(own, after, 2, c, prev_dev)

    def relay(source, c):
        return window_copy(source, relayed, 3, c, mate_dev)

    for c in range(CHUNKS):
        @pl.loop(1, devices)
        def _(k):
            out_copy(k, c).wait_recv()

        permute(place_pick, incoming, own, c)

        @pl.when(has_after)
        def _():
            to_after(c).start()

        @pl.when(has_prev)
        def _():
            to_prev(c).start()

        to_mate(c).start()

    def inverse(ref):
        widened = ref[...].astype(F32)
        return lax.rsqrt(jnp.sum(widened * widened, axis=1, keepdims=True) + EPSILON)

    def visit(j, other, other_inv, other_block):
        other_ids = ids[other_block].astype(F32)
        other_inv_row = as_row(other_inv)

        @in_tiles(rows)
        def _(start, part):
            products = lax.dot_general(
                own[part, :], other[...], (((1,), (1,)), ((), ())), preferred_element_type=F32
            )
            half = products * (own_inv[part, :] * (0.5 * SHARPNESS)) * other_inv_row
            allowed = own_ids[part, :] == other_ids
            if j == 0:
                here = lax.broadcasted_iota(jnp.int32, (TILE, rows), 0) + start
                there = lax.broadcasted_iota(jnp.int32, (TILE, rows), 1)
                allowed = allowed & (here != there)
            scores = jnp.where(allowed, 0.5 + 0.5 * jnp.tanh(half), 0.0)
            weights[part, pl.ds(j * rows, rows)] = scores.astype(BF16)
            counted = jnp.sum(scores, axis=1, keepdims=True)
            if j == 0:
                tally[part, :] = counted
            else:
                tally[part, :] += counted

    def absent(j, other):
        other[...] = jnp.zeros_like(other)
        weights[:, pl.ds(j * rows, rows)] = jnp.zeros((rows, rows), BF16)

    gets_relay = ((core == 0) & has_prev) | ((core == 1) & has_after)

    own_inv[...] = inverse(own)
    visit(0, own, own_inv[...], block)

    for missing, j, ref in (
        (chip == 0, 2, prev),
        (chip == chips - 1, 3, after),
        (((core == 0) & (chip == 0)) | ((core == 1) & (chip == chips - 1)), 4, relayed),
    ):
        @pl.when(missing)
        def _():
            absent(j, ref)

    for c in range(CHUNKS):
        to_mate(c).wait_recv()

    visit(1, mate, inverse(mate), block + 1 - 2 * core)

    for c in range(CHUNKS):
        @pl.when(has_prev)
        def _():
            to_after(c).wait_recv()

            @pl.when(core == 1)
            def _():
                relay(prev, c).start()

        @pl.when(has_after)
        def _():
            to_prev(c).wait_recv()

            @pl.when(core == 0)
            def _():
                relay(after, c).start()

    @pl.when(has_prev)
    def _():
        visit(2, prev, inverse(prev), block - 2)

    @pl.when(has_after)
    def _():
        visit(3, after, inverse(after), block + 2)

    @pl.when(gets_relay)
    def _():
        for c in range(CHUNKS):
            relay(prev, c).wait_recv()

        visit(4, relayed, inverse(relayed), block - 1 + 2 * core)

    tallies[block] = as_row(tally[...])

    def tally_copy(k):
        peer = (me + k) % devices
        return remote(
            tallies.at[block], tallies.at[block], tal_send.at[k], tal_recv.at[k], peer
        )

    def back_copy(k, c):
        peer = (me + k) % devices
        return remote(
            at_slab(returning, peer, c), at_slab(returned, block, c),
            back_send.at[c, k], back_recv.at[c, k], peer,
        )

    for c in range(CHUNKS):
        @in_tiles(rows)
        def _(start, part):
            totals = jnp.dot(weights[part, :], win[:, columns(c)], preferred_element_type=F32)
            emb[part, columns(c)] = (totals * lax.rsqrt(1.0 + tally[part, :])).astype(BF16)

        permute(return_pick, emb, returning, c)

        @pl.loop(1, devices)
        def _(k):
            back_copy(k, c).start()

        at_slab(returned, block, c)[...] = at_slab(returning, me, c)[...]

    @pl.loop(1, devices)
    def _(k):
        tally_copy(k).start()

    @pl.loop(1, devices)
    def _(k):
        tally_copy(k).wait_recv()

    tally_table[...] = jnp.zeros_like(tally_table)

    @pl.loop(0, devices)
    def _(b):
        tally_table[pl.ds(b, 1), :] = tallies[b]

    which = lax.broadcasted_iota(jnp.int32, (128, rows), 0).astype(F32)
    in_block = jnp.dot(
        jnp.transpose(tally_table[...]).astype(BF16),
        ones_where(which == block_row).astype(BF16),
        preferred_element_type=F32,
    )
    inside = pos_row - block_row * rows
    lines = lax.broadcasted_iota(jnp.int32, (rows, rows), 0).astype(F32)
    count_out[...] = jnp.sum(jnp.where(lines == inside, in_block, 0.0), axis=0, keepdims=True)

    for c in range(CHUNKS):
        @pl.loop(1, devices)
        def _(k):
            back_copy(k, c).wait_recv()

        permute(restore_pick, returned, out, c)

    @pl.loop(1, devices)
    def _(k):
        tally_copy(k).wait_send()
        for c in range(CHUNKS):
            out_copy(k, c).wait_send()
            back_copy(k, c).wait_send()

    for c in range(CHUNKS):
        to_mate(c).wait_send()

        @pl.when(has_after)
        def _():
            to_after(c).wait_send()

        @pl.when(has_prev)
        def _():
            to_prev(c).wait_send()

        @pl.when(((core == 1) & has_prev) | ((core == 0) & has_after))
        def _():
            relay(prev, c).wait_send()


def local(embeddings, position, member, cluster):
    rows, width = embeddings.shape
    devices = lax.axis_size("blk")
    slab = max(16, rows // devices)
    slots = devices * slab
    vmem = pl.BlockSpec(memory_space=pltpu.VMEM)
    dma = pltpu.SemaphoreType.DMA
    smoothed, counts = pl.pallas_call(
        functools.partial(kernel, devices, slab),
        out_shape=(
            jax.ShapeDtypeStruct((rows, width), BF16),
            jax.ShapeDtypeStruct((1, rows), F32),
        ),
        in_specs=[pl.BlockSpec(memory_space=pl.ANY), vmem, vmem, vmem],
        out_specs=(vmem, vmem),
        scratch_shapes=[
            pltpu.VMEM((rows, width), BF16),
            pltpu.VMEM((slots, width), BF16),
            pltpu.VMEM((slots, width), BF16),
            pltpu.VMEM((5 * rows, width), BF16),
            pltpu.VMEM((rows, 5 * rows), BF16),
            pltpu.VMEM((slots, width), BF16),
            pltpu.VMEM((slots, width), BF16),
            pltpu.VMEM((slots, rows), BF16),
            pltpu.VMEM((rows, slots), BF16),
            pltpu.VMEM((rows, slots), BF16),
            pltpu.VMEM((slots, rows), BF16),
            pltpu.VMEM((devices, 1, rows), F32),
            pltpu.VMEM((128, rows), F32),
            pltpu.VMEM((rows, 1), F32),
            pltpu.VMEM((rows, 1), F32),
            pltpu.VMEM((rows, 1), F32),
            pltpu.VMEM((1, rows), jnp.int32),
            dma,
            dma((2,)),
            dma((CHUNKS, devices)),
            dma((CHUNKS, devices)),
            dma((4, CHUNKS)),
            dma((4, CHUNKS)),
            dma((CHUNKS, devices)),
            dma((CHUNKS, devices)),
            dma((devices,)),
            dma((devices,)),
        ],
        compiler_params=pltpu.CompilerParams(
            collective_id=0, has_side_effects=True, vmem_limit_bytes=48 * 1024 * 1024
        ),
    )(
        embeddings,
        position.reshape(1, rows),
        member.reshape(1, rows),
        cluster.reshape(devices, 1, rows),
    )
    return smoothed, counts.reshape(rows).astype(BF16)


def solution(mesh):
    in_specs = (P(("groups", "blk"), None), P(("groups", "blk")), P(("groups", "blk")), P("groups"))
    out_specs = (P(("groups", "blk"), None), P(("groups", "blk")))
    return jax.shard_map(local, mesh=mesh, in_specs=in_specs, out_specs=out_specs, check_vma=False)
```

time: 91 us -> 90.8 us (level)
  the two profiles are of different devices: /device:TPU:13 before, /device:TPU:0 now
where the time goes in v2:
time: 90.8 us; the launch traced here: 90.6 us
  Pallas kernels  85.7 us (94%)
  local copies, waits for them, and re-layouts  3.63 us (4%)
    pallas_call x1, Pallas kernels, local(): pl.pallas_call(functools.partial(kernel, devices, slab), out_shape=(jax.S...  85.7 us
    unnamed x9, local copies, waits for them, and re-layouts  3.63 us

profile of v2, /device:TPU:0, one launch (start us, length us, event | category | flops | bytes accessed | tf_op | source)
XLA Modules:
  0.0 90.6 jit_solution(14021582792074836015)
XLA Ops:
  0.6 0.0 copy-start.3
  0.6 0.0 copy-start.2
  0.7 0.7 copy-done.3
  1.3 0.0 copy-done.2
  1.3 0.0 copy-start
  1.3 1.2 %copy-done = bf16[512,1024]{1,0:T(8,128)(2,1)S(1)} copy-done((bf16[512,1024]{1,0:T(8,128)(2,1)S(1)}, bf16[512,1024]{1,0:T(8,128)(2,1)}, u32[]{:S(2)}) %copy-start) | copy-done | bytes 1048600
  2.6 0.0 copy-start.1
  2.6 0.8 copy-done.1
  3.3 85.7 %shard_map.59 = (bf16[512,1024]{1,0:T(8,128)(2,1)S(1)}, f32[1,512]{1,0:T(1,128)S(1)}) custom-call(bf16[512,1024]{1,0:T(8,128)(2,1)S(1)} %copy-done, s32[1,512]{1,0:T(1,128)S(1)} %bitcast.4, s32[1,512]{1,0:T(1,128)S(1)} %bitcast.5, s32[16,1,512]{2,1,0:T(1,128)S(1)} %bitcast.3), custom_call_target="tpu_custom_call" | custom-call | tf_op jit(solution)/shard_map/pallas_call | solution.py:367
  89.0 0.6 convert_reduce_fusion
  89.6 1.0 %copy.7 = bf16[512,1024]{1,0:T(8,128)(2,1)} copy(bf16[512,1024]{1,0:T(8,128)(2,1)S(1)} %get-tuple-element.8) | data formatting | bytes 2097152
Async XLA Ops:
  0.6 0.7 copy-start.3
  0.6 0.7 copy-start.2
  1.3 1.2 %copy-start = (bf16[512,1024]{1,0:T(8,128)(2,1)S(1)}, bf16[512,1024]{1,0:T(8,128)(2,1)}, u32[]{:S(2)}) copy-start(bf16[512,1024]{1,0:T(8,128)(2,1)} %emb_hbm.1) | copy-start | bytes 3145732
  2.6 0.8 copy-start.1

commit v3 on v2

--- a/solution.py
+++ b/solution.py
@@ -9,8 +9,8 @@
 
 SHARPNESS = 32.0
 EPSILON = 1e-06
-TILE = 256
-CHUNKS = 4
+TILE = 512
+CHUNKS = 2
 F32 = jnp.float32
 BF16 = jnp.bfloat16
 

time: 90.8 us -> 87.8 us (0.967)
  Pallas kernels: 85.7 us -> 82.7 us
    pallas_call x1, Pallas kernels: 85.7 us -> 82.7 us  [local(): pl.pallas_call(functools.partial(kernel, devices, slab), out_shape=(jax.S...]
where the time goes in v3:
time: 87.8 us; the launch traced here: 87.6 us
  Pallas kernels  82.7 us (94%)
  local copies, waits for them, and re-layouts  3.63 us (4%)
    pallas_call x1, Pallas kernels, local(): pl.pallas_call(functools.partial(kernel, devices, slab), out_shape=(jax.S...  82.7 us
    unnamed x9, local copies, waits for them, and re-layouts  3.63 us

profile of v3, /device:TPU:0, one launch (start us, length us, event | category | flops | bytes accessed | tf_op | source)
XLA Modules:
  0.0 87.6 jit_solution(10285022209185556570)
XLA Ops:
  0.6 0.0 copy-start.3
  0.6 0.0 copy-start.2
  0.7 0.7 copy-done.3
  1.3 0.0 copy-done.2
  1.3 0.0 copy-start
  1.3 1.2 %copy-done = bf16[512,1024]{1,0:T(8,128)(2,1)S(1)} copy-done((bf16[512,1024]{1,0:T(8,128)(2,1)S(1)}, bf16[512,1024]{1,0:T(8,128)(2,1)}, u32[]{:S(2)}) %copy-start) | copy-done | bytes 1048600
  2.6 0.0 copy-start.1
  2.6 0.8 copy-done.1
  3.3 82.7 %shard_map.59 = (bf16[512,1024]{1,0:T(8,128)(2,1)S(1)}, f32[1,512]{1,0:T(1,128)S(1)}) custom-call(bf16[512,1024]{1,0:T(8,128)(2,1)S(1)} %copy-done, s32[1,512]{1,0:T(1,128)S(1)} %bitcast.4, s32[1,512]{1,0:T(1,128)S(1)} %bitcast.5, s32[16,1,512]{2,1,0:T(1,128)S(1)} %bitcast.3), custom_call_target="tpu_custom_call" | custom-call | tf_op jit(solution)/shard_map/pallas_call | solution.py:367
  86.0 0.6 convert_reduce_fusion
  86.6 1.0 %copy.7 = bf16[512,1024]{1,0:T(8,128)(2,1)} copy(bf16[512,1024]{1,0:T(8,128)(2,1)S(1)} %get-tuple-element.8) | data formatting | bytes 2097152
Async XLA Ops:
  0.6 0.7 copy-start.3
  0.6 0.7 copy-start.2
  1.3 1.2 %copy-start = (bf16[512,1024]{1,0:T(8,128)(2,1)S(1)}, bf16[512,1024]{1,0:T(8,128)(2,1)}, u32[]{:S(2)}) copy-start(bf16[512,1024]{1,0:T(8,128)(2,1)} %emb_hbm.1) | copy-start | bytes 3145732
  2.6 0.8 copy-start.1

commit v4 on v3

--- a/solution.py
+++ b/solution.py
@@ -402,7 +402,7 @@
             dma((devices,)),
         ],
         compiler_params=pltpu.CompilerParams(
-            collective_id=0, has_side_effects=True, vmem_limit_bytes=48 * 1024 * 1024
+            collective_id=0, has_side_effects=True, vmem_limit_bytes=63 * 1024 * 1024
         ),
     )(
         embeddings,

time: 87.8 us -> 88.7 us (1.010)
  Pallas kernels: 82.7 us -> 84.3 us
    pallas_call x1, Pallas kernels: 82.7 us -> 84.3 us  [local(): pl.pallas_call(functools.partial(kernel, devices, slab), out_shape=(jax.S...]
    unnamed x9 -> x3, local copies, waits for them, and re-layouts: 3.63 us -> 2.93 us
where the time goes in v4:
time: 88.7 us; the launch traced here: 88.4 us
  Pallas kernels  84.3 us (95%)
  local copies, waits for them, and re-layouts  2.93 us (3%)
    pallas_call x1, Pallas kernels, local(): pl.pallas_call(functools.partial(kernel, devices, slab), out_shape=(jax.S...  84.3 us
    unnamed x3, local copies, waits for them, and re-layouts  2.93 us

profile of v4, /device:TPU:0, one launch (start us, length us, event | category | flops | bytes accessed | tf_op | source)
XLA Modules:
  0.0 88.4 jit_solution(11991343716423033737)
XLA Ops:
  0.6 84.3 %shard_map.59 = (bf16[512,1024]{1,0:T(8,128)(2,1)}, f32[1,512]{1,0:T(1,128)}) custom-call(bf16[512,1024]{1,0:T(8,128)(2,1)} %emb_hbm.1, s32[1,512]{1,0:T(1,128)} %bitcast.4, s32[1,512]{1,0:T(1,128)} %bitcast.5, s32[16,1,512]{2,1,0:T(1,128)} %bitcast.3), custom_call_target="tpu_custom_call" | custom-call | tf_op jit(solution)/shard_map/pallas_call | solution.py:367
  84.9 0.0 copy-start
  84.9 0.7 copy-done
  85.6 0.6 convert_reduce_fusion
  86.2 2.3 %copy.7 = bf16[512,1024]{1,0:T(8,128)(2,1)} copy(bf16[512,1024]{1,0:T(8,128)(2,1)} %get-tuple-element.8) | data formatting | bytes 2097152
Async XLA Ops:
  84.9 0.7 copy-start
